TPU v7x, 512 devices: a whole 4x8x8 slice. The times are simulated.
512 devices in a mesh: gx: 16 (over z, core), gy: 32 (over y, x).
Axes of the slice: x: 4, y: 8, z: 8, core: 2. Of those that a mesh axis runs over, the one named last changes fastest.
Arguments:
- unary_score: bfloat16 [64, 256, 512], P('gx', 'gy'), may hold values from -12 to 400
- affinity: bfloat16 [64, 256, 1664], P('gx', 'gy'), may hold values from 0.099609375 to 1
- compatibility: float32 [8, 8], replicated, may hold values from -3 to 3
- kernel: float32 [26], replicated, may hold values from 0.05 to 0.4
- cotangent: bfloat16 [64, 256, 512], P('gx', 'gy'), may hold values from -8 to 8
Outputs:
- grad_unary: bfloat16 [64, 256, 512], P('gx', 'gy')
- grad_affinity: bfloat16 [64, 256, 1664], P('gx', 'gy')
- grad_compat: float32 [8, 8], replicated
- grad_kernel: float32 [26], replicated
All inputs are finite; a program needn't handle non-finite values.
Results may differ from a plain program's by a relative error of at most 0.0045.
Values may be sent and summed in bfloat16 or wider, within the bound.
A program may use at most 128 MiB of HBM per device.

v0:
```python
import functools
import math

import jax
import jax.numpy as jnp
from jax import lax
from jax.experimental import pallas as pl
from jax.experimental.pallas import tpu as pltpu
from jax.sharding import PartitionSpec as P

LABELS = 8
DEPTH = 64
NEIGH = 26
ITERS = 3

OFFSETS = [
    (step_x, step_y, step_z)
    for step_x in (-1, 0, 1)
    for step_y in (-1, 0, 1)
    for step_z in (-1, 0, 1)
    if (step_x, step_y, step_z) != (0, 0, 0)
]
NUMBER = {offset: number for number, offset in enumerate(OFFSETS)}

SPAN = 12
TALL = 24
BASE = 8
DIRECTIONS = [(-1, 0), (1, 0), (0, -1), (0, 1), (-1, -1), (-1, 1), (1, -1), (1, 1)]
WIDE = 32
MESH = pl.DeviceIdType.MESH


def low_half():
    return lax.broadcasted_iota(jnp.int32, (8, 128), 1) < DEPTH


def swap(values):
    return pltpu.roll(values, DEPTH, values.ndim - 1)


def inner_rows(y, p, label, width):
    return pl.ds(((y + 2) * 2 + p) * width + label, 8, stride=2 * width)


def side_rows(y, label, width):
    return pl.ds((y + 2) * width + label, 8, stride=width)


def spread(source, tiles, put):
    low = low_half()
    for tile in range(tiles):
        cols = [
            source[x, :, 128 * tile : 128 * (tile + 1)].astype(jnp.float32) for x in range(4)
        ]
        turned = [swap(col) for col in cols]
        for p in (0, 1):
            put(2 * tile, p, jnp.where(low, cols[p], turned[p + 2]))
            put(2 * tile + 1, p, jnp.where(low, turned[p], cols[p + 2]))


def gather_columns(values, tiles, put):
    low = low_half()
    for tile in range(tiles):
        for p in (0, 1):
            even, odd = values(2 * tile, p), values(2 * tile + 1, p)
            put(tile, p, jnp.where(low, even, swap(odd)))
            put(tile, p + 2, jnp.where(low, swap(even), odd))


def lay_out(inner, sides, width, label, first, second):
    low = low_half()
    inner[inner_rows(0, 0, label, width), :] = first
    inner[inner_rows(0, 1, label, width), :] = second
    sides[pl.ds(label, 8, stride=width), :] = jnp.where(low, first, swap(second))
    sides[pl.ds(8 * width + label, 8, stride=width), :] = jnp.where(low, swap(first), second)


def assemble(inner, minus, plus, width, label, y, reach):
    low = low_half()
    own = [inner[inner_rows(y, p, label, width), :] for p in (0, 1)]
    before = minus[side_rows(y, label, width), :]
    after = plus[side_rows(y, label, width), :]
    found = {0: own[0], 1: own[1]}
    found[2] = swap(jnp.where(low, after, own[0]))
    found[-1] = swap(jnp.where(low, own[1], before))
    if reach == 2:
        found[3] = jnp.where(low, swap(own[1]), after)
        found[-2] = jnp.where(low, before, swap(own[0]))
    return found


def message(weight, field, columns, y):
    sums = {p: None for p in columns}
    for step_y in (-1, 0, 1):
        for step_z in (-1, 0, 1):
            for source in range(min(columns) - 1, max(columns) + 2):
                users = [
                    (source - step_x, NUMBER[(step_x, step_y, step_z)])
                    for step_x in (-1, 0, 1)
                    if source - step_x in sums and (step_x, step_y, step_z) in NUMBER
                ]
                if not users:
                    continue
                near = field[step_z + 1, :, source + 2, pl.ds(BASE + y + step_y, 8), :]
                for p, number in users:
                    term = weight(number, p)[None] * near
                    sums[p] = term if sums[p] is None else sums[p] + term
    return sums


def mix(coef, values):
    rows = []
    for a in range(LABELS):
        total = coef(a, 0) * values[0]
        for b in range(1, LABELS):
            total = total + coef(a, b) * values[b]
        rows.append(total)
    return jnp.stack(rows)


def normalise(logits):
    powers = jnp.exp(logits - jnp.max(logits, axis=0, keepdims=True))
    return powers / jnp.sum(powers, axis=0, keepdims=True)


def softmax_back(current, grad_in):
    return current * (grad_in - jnp.sum(current * grad_in, axis=0, keepdims=True))


def put_field(field, label, p, y, value):
    axis = value.ndim - 1
    field[1, label, p + 2, pl.ds(BASE + y, 8), :] = value
    field[0, label, p + 2, pl.ds(BASE + y, 8), :] = pltpu.roll(value, 1, axis)
    field[2, label, p + 2, pl.ds(BASE + y, 8), :] = pltpu.roll(value, 127, axis)


def kernel(
    sizes,
    unary_hbm,
    affinity_hbm,
    cotangent_hbm,
    compat,
    strength,
    grad_unary_hbm,
    grad_affinity_hbm,
    grad_compat,
    grad_kernel,
    unary_in,
    affinity_in,
    cotangent_in,
    unary_out,
    affinity_out,
    inner_u,
    sides_u,
    minus_u,
    plus_u,
    inner_a,
    sides_a,
    minus_a,
    plus_a,
    inner_send,
    sides_send,
    inner_recv,
    minus_recv,
    plus_recv,
    inner_q,
    sides_q,
    minus_q,
    plus_q,
    inner_g,
    sides_g,
    minus_g,
    plus_g,
    inner_h,
    sides_h,
    minus_h,
    plus_h,
    logits,
    own_grad,
    field_0,
    field_1,
    field_2,
    field_g,
    field_h,
    field_i,
    wide_aff,
    weight_own,
    weight_rim,
    weight_back,
    message_1,
    message_2,
    rim_p,
    total_u,
    total_c,
    total_r,
    gather_a,
    gather_b,
    gather_c,
    load_sem,
    store_sem,
    halo_send,
    halo_recv,
    peer_send,
    peer_recv,
):
    size_gx, size_gy, size_far, size_near = sizes
    me_x, me_y = lax.axis_index("gx"), lax.axis_index("gy")
    me_far, me_near = me_y // size_near, lax.rem(me_y, size_near)
    low = low_half()

    def around(index, step, size):
        return lax.rem(index + (step + size), size)

    loads = [
        pltpu.make_async_copy(unary_hbm, unary_in, load_sem.at[0]),
        pltpu.make_async_copy(affinity_hbm, affinity_in, load_sem.at[1]),
        pltpu.make_async_copy(cotangent_hbm, cotangent_in, load_sem.at[2]),
    ]
    for load in loads:
        load.start()

    neighbours = [
        (around(me_x, step_x, size_gx), around(me_y, step_y, size_gy))
        for step_x, step_y in DIRECTIONS
    ]
    peers_a = [(around(me_x, step, size_gx), me_y) for step in range(1, size_gx)]
    peers_b = [
        (me_x, around(me_far, step, size_far) * size_near + me_near)
        for step in range(1, size_far)
    ]
    peers_c = [
        (me_x, me_far * size_near + around(me_near, step, size_near))
        for step in range(1, size_near)
    ]
    everyone = neighbours + peers_a + peers_b + peers_c
    barrier = pltpu.get_barrier_semaphore()
    for device in everyone:
        pl.semaphore_signal(barrier, inc=1, device_id=device, device_id_type=MESH)

    def exchange(number, width, reach, inner, sides, minus, plus):
        copies = []
        for d, (step_x, step_y) in enumerate(DIRECTIONS):
            if step_x == 0:
                first = 2 if step_y < 0 else 10 - reach
                land = 10 if step_y < 0 else 2 - reach
                source = inner.at[pl.ds(first * 2 * width, reach * 2 * width), :]
                target = inner.at[pl.ds(land * 2 * width, reach * 2 * width), :]
            else:
                base = 0 if step_x < 0 else 8 * width
                landing = plus if step_x < 0 else minus
                if step_y == 0:
                    source = sides.at[pl.ds(base, 8 * width), :]
                    target = landing.at[pl.ds(2 * width, 8 * width), :]
                else:
                    first = 0 if step_y < 0 else 8 - reach
                    land = 10 if step_y < 0 else 2 - reach
                    source = sides.at[pl.ds(base + first * width, reach * width), :]
                    target = landing.at[pl.ds(land * width, reach * width), :]
            copies.append(remote(number, d, source, target))
        for copy in copies:
            copy.start()
        return copies

    def remote(number, d, source, target):
        return pltpu.make_async_remote_copy(
            src_ref=source,
            dst_ref=target,
            send_sem=halo_send.at[number, d],
            recv_sem=halo_recv.at[number, d],
            device_id=neighbours[d],
            device_id_type=MESH,
        )

    def arrive(copies):
        for copy in copies:
            copy.wait_recv()

    lane = lax.broadcasted_iota(jnp.int32, (8, 128), 1)
    depth = lax.rem(lane, DEPTH)
    half = lane // DEPTH
    sublane = lax.broadcasted_iota(jnp.int32, (8, 128), 0)

    def inside(position, size):
        return jnp.where((position >= 0) & (position < size), 1.0, 0.0)

    mask_z = {step: inside(depth + step, DEPTH) for step in (-1, 0, 1)}
    mask_x = {at: inside(me_x * 4 + at + 2 * half, 4 * size_gx) for at in range(-2, 4)}

    def mask_y(y):
        return inside(me_y * 8 + y + sublane, 8 * size_gy)

    loads[0].wait()
    held = {}

    def keep(label, p, value):
        held[(label, p)] = value
        logits[label, p + 2, pl.ds(BASE, 8), :] = value
        if p == 1:
            lay_out(inner_u, sides_u, LABELS, label, held[(label, 0)], value)

    spread(unary_in, 4, keep)
    pl.semaphore_wait(barrier, len(everyone))
    sent_u = exchange(0, LABELS, 1, inner_u, sides_u, minus_u, plus_u)

    loads[1].wait()
    mask_own_y = {step: mask_y(step) for step in (-1, 0, 1)}

    def keep_affinity(number, p, value):
        held[(number, p)] = value
        step_x, step_y, step_z = OFFSETS[number]
        mask = mask_x[p + step_x] * mask_own_y[step_y] * mask_z[step_z]
        weight_own[number, p] = value * mask * strength[number]
        if p == 1:
            lay_out(inner_a, sides_a, WIDE, number, held[(number, 0)], value)

    spread(affinity_in, NEIGH // 2, keep_affinity)
    nothing = jnp.zeros((8, 128), jnp.float32)
    for number in range(NEIGH, WIDE):
        lay_out(inner_a, sides_a, WIDE, number, nothing, nothing)
    edge = 2 * 2 * WIDE
    inner_send[0:edge, :] = inner_a[edge : 2 * edge, :].astype(jnp.bfloat16)
    inner_send[edge : 2 * edge, :] = inner_a[4 * edge : 5 * edge, :].astype(jnp.bfloat16)
    sides_send[...] = sides_a[...].astype(jnp.bfloat16)
    copies_a = []
    for d, (step_x, step_y) in enumerate(DIRECTIONS):
        if step_x == 0:
            part = pl.ds(0 if step_y < 0 else edge, edge)
            source, target = inner_send.at[part, :], inner_recv.at[part, :]
        else:
            start = 0 if step_x < 0 else 8 * WIDE
            landing = plus_recv if step_x < 0 else minus_recv
            if step_y == 0:
                source = sides_send.at[pl.ds(start, 8 * WIDE), :]
                target = landing.at[pl.ds(2 * WIDE, 8 * WIDE), :]
            else:
                first = 0 if step_y < 0 else 6
                land = 10 if step_y < 0 else 0
                source = sides_send.at[pl.ds(start + first * WIDE, 2 * WIDE), :]
                target = landing.at[pl.ds(land * WIDE, 2 * WIDE), :]
        copies_a.append(remote(1, d, source, target))
    for copy in copies_a:
        copy.start()

    arrive(sent_u)
    for label in range(LABELS):
        for y in (-1, 1):
            found = assemble(inner_u, minus_u, plus_u, LABELS, label, y, 1)
            for p in (-1, 0, 1, 2):
                logits[label, p + 2, pl.ds(BASE + y, 8), :] = found[p]
    for y in (-1, 1):
        for p in (-1, 0, 1, 2):
            value = normalise(logits[:, p + 2, pl.ds(BASE + y, 8), :])
            put_field(field_0, slice(None), p, y, value)

    def own_logits(p):
        return logits[:, p + 2, pl.ds(BASE, 8), :]

    def own_weight(number, p):
        return weight_own[number, p]

    def forward(a, b):
        return compat[a, b]

    def backward(b, a):
        return compat[a, b]

    def send_field(number, reach, values, inner, sides, minus, plus):
        for label in range(LABELS):
            lay_out(inner, sides, LABELS, label, values[0][label], values[1][label])
        return exchange(number, LABELS, reach, inner, sides, minus, plus)

    sums = message(own_weight, field_0, (0, 1), 0)
    values = []
    for p in (0, 1):
        message_1[:, p] = sums[p]
        values.append(normalise(own_logits(p) - mix(forward, sums[p])))
    sent_q = send_field(2, 2, values, inner_q, sides_q, minus_q, plus_q)

    loads[2].wait()

    def keep_cotangent(label, p, value):
        own_grad[label, p] = value

    spread(cotangent_in, 4, keep_cotangent)
    arrive(copies_a)
    inner_a[0:edge, :] = inner_recv[edge : 2 * edge, :].astype(jnp.float32)
    inner_a[5 * edge : 6 * edge, :] = inner_recv[0:edge, :].astype(jnp.float32)
    minus_a[...] = minus_recv[...].astype(jnp.float32)
    plus_a[...] = plus_recv[...].astype(jnp.float32)
    for number in range(NEIGH):
        for y in (-2, 2):
            found = assemble(inner_a, minus_a, plus_a, WIDE, number, y, 2)
            for p in range(-2, 4):
                wide_aff[number, p + 2, pl.ds(BASE + y, 8), :] = found[p] * strength[number]
    rim_mask_y = {y: mask_y(y) for y in (-2, -1, 0, 1, 2)}

    def rim_weights(target, value):
        for y in (-1, 1):
            for p in (-1, 0, 1, 2):
                for number, (step_x, step_y, step_z) in enumerate(OFFSETS):
                    across = mask_x[p + step_x] * rim_mask_y[y + step_y]
                    if step_z != 0:
                        across = across * mask_z[step_z]
                    target[number, p + 1, pl.ds(BASE + y, 8), :] = across * value(number, p, y)

    def rim_value(number, p, y):
        return wide_aff[number, p + 2, pl.ds(BASE + y, 8), :]

    def back_value(number, p, y):
        step_x, step_y, step_z = OFFSETS[number]
        opposite = NUMBER[(-step_x, -step_y, -step_z)]
        value = wide_aff[opposite, p + step_x + 2, pl.ds(BASE + y + step_y, 8), :]
        if step_z != 0:
            value = pltpu.roll(value, (128 - step_z) % 128, 1)
        return value

    rim_weights(weight_rim, rim_value)

    arrive(sent_q)
    for label in range(LABELS):
        for y in (-2, 2):
            found = assemble(inner_q, minus_q, plus_q, LABELS, label, y, 2)
            for p in range(-2, 4):
                put_field(field_1, label, p, y, found[p])
    for y in (-1, 1):

        def rim_weight(number, p, y=y):
            return weight_rim[number, p + 1, pl.ds(BASE + y, 8), :]

        sums = message(rim_weight, field_1, (-1, 0, 1, 2), y)
        for p in (-1, 0, 1, 2):
            message_2[:, p + 1, pl.ds(BASE + y, 8), :] = sums[p]
            here = logits[:, p + 2, pl.ds(BASE + y, 8), :]
            put_field(field_2, slice(None), p, y, normalise(here - mix(forward, sums[p])))

    sums = message(own_weight, field_2, (0, 1), 0)
    grads = []
    values = []
    for p in (0, 1):
        current = normalise(own_logits(p) - mix(forward, sums[p]))
        step = softmax_back(current, own_grad[:, p])
        total_u[:, p] = step
        grads.append(-step)
        values.append(mix(backward, -step))
    sent_g = send_field(3, 2, values, inner_g, sides_g, minus_g, plus_g)

    def add_compat(grads, messages, begin):
        for b in range(LABELS):
            term = grads[0] * messages[0][b][None] + grads[1] * messages[1][b][None]
            total_c[b] = term if begin else total_c[b] + term

    def add_kernel(values, field, begin):
        for number, (step_x, step_y, step_z) in enumerate(OFFSETS):
            for p in (0, 1):
                near = field[step_z + 1, :, p + step_x + 2, pl.ds(BASE + step_y, 8), :]
                joint = jnp.sum(values[p] * near, axis=0)
                total_r[number, p] = joint if begin else total_r[number, p] + joint

    add_compat(grads, [sums[0], sums[1]], True)
    add_kernel(values, field_2, True)
    rim_weights(weight_back, back_value)

    arrive(sent_g)
    for label in range(LABELS):
        for y in (-2, 2):
            found = assemble(inner_g, minus_g, plus_g, LABELS, label, y, 2)
            for p in range(-2, 4):
                put_field(field_g, label, p, y, found[p])

    def back_weight_at(y):
        def back_weight(number, p):
            return weight_back[number, p + 1, pl.ds(BASE + y, 8), :]

        return back_weight

    for y in (-1, 1):
        sums = message(back_weight_at(y), field_g, (-1, 0, 1, 2), y)
        for p in (-1, 0, 1, 2):
            current = field_2[1, :, p + 2, pl.ds(BASE + y, 8), :]
            grad_p = -softmax_back(current, sums[p])
            rim_p[:, p + 1, pl.ds(BASE + y, 8), :] = grad_p
            put_field(field_h, slice(None), p, y, mix(backward, grad_p))

    sums = message(back_weight_at(0), field_h, (0, 1), 0)
    grads_1 = []
    values_1 = []
    for p in (0, 1):
        current = field_1[1, :, p + 2, pl.ds(BASE, 8), :]
        step = softmax_back(current, sums[p])
        total_u[:, p] = total_u[:, p] + step
        grads_1.append(-step)
        values_1.append(mix(backward, -step))
    sent_h = send_field(4, 1, values_1, inner_h, sides_h, minus_h, plus_h)

    grads_2 = [rim_p[:, p + 1, pl.ds(BASE, 8), :] for p in (0, 1)]
    for p in (0, 1):
        total_u[:, p] = total_u[:, p] - grads_2[p]
    add_compat(grads_2, [message_2[:, p + 1, pl.ds(BASE, 8), :] for p in (0, 1)], False)
    add_kernel([field_h[1, :, p + 2, pl.ds(BASE, 8), :] for p in (0, 1)], field_1, False)
    add_compat(grads_1, [message_1[:, p] for p in (0, 1)], False)
    add_kernel(values_1, field_0, False)

    local = jnp.zeros((8, 128), jnp.float32)
    for b in range(LABELS):
        total = jnp.sum(jnp.sum(total_c[b], axis=1), axis=1, keepdims=True)
        local = jnp.where(lane == b, total, local)
    joint_rows = []
    for number, (step_x, step_y, step_z) in enumerate(OFFSETS):
        row = None
        for p in (0, 1):
            mask = mask_x[p + step_x] * mask_own_y[step_y] * mask_z[step_z]
            joint = total_r[number, p] * mask
            total_r[number, p] = joint * strength[number]
            term = joint * inner_a[inner_rows(0, p, number, WIDE), :]
            row = term if row is None else row + term
        joint_rows.append(jnp.sum(row, axis=0, keepdims=True))
    for group in range(4):
        rows = joint_rows[8 * group : 8 * (group + 1)]
        rows = rows + [jnp.zeros((1, 128), jnp.float32)] * (8 - len(rows))
        total = jnp.sum(jnp.concatenate(rows, axis=0), axis=1, keepdims=True)
        local = jnp.where(lane == LABELS + group, total, local)

    def share(buffer, me, peers, base, value):
        buffer[me] = value
        copies = [
            pltpu.make_async_remote_copy(
                src_ref=buffer.at[me],
                dst_ref=buffer.at[me],
                send_sem=peer_send.at[base + place],
                recv_sem=peer_recv.at[base + place],
                device_id=device,
                device_id_type=MESH,
            )
            for place, device in enumerate(peers)
        ]
        for copy in copies:
            copy.start()
        return copies

    def collect(buffer, copies):
        arrive(copies)
        total = buffer[0]
        for place in range(1, buffer.shape[0]):
            total = total + buffer[place]
        return total

    shared_a = share(gather_a, me_x, peers_a, 0, local)

    def put_affinity(tile, x, value):
        affinity_out[x, :, 128 * tile : 128 * (tile + 1)] = value.astype(jnp.bfloat16)

    gather_columns(lambda number, p: total_r[number, p], NEIGH // 2, put_affinity)
    store_a = pltpu.make_async_copy(affinity_out, grad_affinity_hbm, store_sem.at[0])
    store_a.start()

    arrive(sent_h)
    for label in range(LABELS):
        for y in (-1, 1):
            found = assemble(inner_h, minus_h, plus_h, LABELS, label, y, 1)
            for p in (-1, 0, 1, 2):
                put_field(field_i, label, p, y, found[p])
    shared_b = share(gather_b, me_far, peers_b, len(peers_a), collect(gather_a, shared_a))
    sums = message(back_weight_at(0), field_i, (0, 1), 0)
    for p in (0, 1):
        current = field_0[1, :, p + 2, pl.ds(BASE, 8), :]
        total_u[:, p] = total_u[:, p] + softmax_back(current, sums[p])

    def put_unary(tile, x, value):
        unary_out[x, :, 128 * tile : 128 * (tile + 1)] = value.astype(jnp.bfloat16)

    gather_columns(lambda label, p: total_u[label, p], LABELS // 2, put_unary)
    store_u = pltpu.make_async_copy(unary_out, grad_unary_hbm, store_sem.at[1])
    store_u.start()

    shared_c = share(
        gather_c, me_near, peers_c, len(peers_a) + len(peers_b), collect(gather_b, shared_b)
    )
    voxels = size_gx * 4 * size_gy * 8 * DEPTH
    final = collect(gather_c, shared_c) * (1.0 / math.sqrt(voxels))
    grad_compat[...] = final[:, :LABELS]
    picked = jnp.zeros((8, 128), jnp.float32)
    for group in range(4):
        wanted = lane == 8 * group + sublane
        picked = jnp.where(wanted, final[:, LABELS + group : LABELS + group + 1], picked)
    grad_kernel[...] = jnp.sum(picked, axis=0, keepdims=True)[:, :NEIGH]

    for copy in sent_u + copies_a + sent_q + sent_g + sent_h + shared_a + shared_b + shared_c:
        copy.wait_send()
    store_a.wait()
    store_u.wait()


def shards(sizes, unary_score, affinity, compatibility, kernel_weights, cotangent):
    size_gx, size_gy, size_far, size_near = sizes
    f32, bf16 = jnp.float32, jnp.bfloat16

    def rows(count, kind=f32):
        return pltpu.VMEM((count, 128), kind)

    def exchanged(width):
        return [
            rows(SPAN * 2 * width),
            rows(2 * 8 * width),
            rows(SPAN * width),
            rows(SPAN * width),
        ]

    field = pltpu.VMEM((3, LABELS, 6, TALL, 128), f32)
    pair = pltpu.VMEM((LABELS, 2, 8, 128), f32)
    rim = pltpu.VMEM((LABELS, 4, TALL, 128), f32)
    peers = size_gx + size_far + size_near - 3
    scratch = (
        [
            pltpu.VMEM(unary_score.shape, bf16),
            pltpu.VMEM(affinity.shape, bf16),
            pltpu.VMEM(cotangent.shape, bf16),
            pltpu.VMEM(unary_score.shape, bf16),
            pltpu.VMEM(affinity.shape, bf16),
        ]
        + exchanged(LABELS)
        + exchanged(WIDE)
        + [
            rows(2 * 4 * WIDE, bf16),
            rows(2 * 8 * WIDE, bf16),
            rows(2 * 4 * WIDE, bf16),
            rows(SPAN * WIDE, bf16),
            rows(SPAN * WIDE, bf16),
        ]
        + exchanged(LABELS)
        + exchanged(LABELS)
        + exchanged(LABELS)
        + [
            pltpu.VMEM((LABELS, 6, TALL, 128), f32),
            pair,
            field,
            field,
            field,
            field,
            field,
            field,
            pltpu.VMEM((NEIGH, 6, TALL, 128), f32),
            pltpu.VMEM((NEIGH, 2, 8, 128), f32),
            pltpu.VMEM((NEIGH, 4, TALL, 128), f32),
            pltpu.VMEM((NEIGH, 4, TALL, 128), f32),
            pair,
            rim,
            rim,
            pair,
            pltpu.VMEM((LABELS, LABELS, 8, 128), f32),
            pltpu.VMEM((NEIGH, 2, 8, 128), f32),
            pltpu.VMEM((size_gx, 8, 128), f32),
            pltpu.VMEM((size_far, 8, 128), f32),
            pltpu.VMEM((size_near, 8, 128), f32),
            pltpu.SemaphoreType.DMA((3,)),
            pltpu.SemaphoreType.DMA((2,)),
            pltpu.SemaphoreType.DMA((5, 8)),
            pltpu.SemaphoreType.DMA((5, 8)),
            pltpu.SemaphoreType.DMA((peers,)),
            pltpu.SemaphoreType.DMA((peers,)),
        ]
    )
    anywhere = pl.BlockSpec(memory_space=pl.ANY)
    scalars = pl.BlockSpec(memory_space=pltpu.SMEM)
    vectors = pl.BlockSpec(memory_space=pltpu.VMEM)
    grad_unary, grad_affinity, grad_compat, grad_kernel = pl.pallas_call(
        functools.partial(kernel, sizes),
        out_shape=(
            jax.ShapeDtypeStruct(unary_score.shape, bf16),
            jax.ShapeDtypeStruct(affinity.shape, bf16),
            jax.ShapeDtypeStruct((LABELS, LABELS), f32),
            jax.ShapeDtypeStruct((1, NEIGH), f32),
        ),
        in_specs=[anywhere, anywhere, anywhere, scalars, scalars],
        out_specs=(anywhere, anywhere, vectors, vectors),
        scratch_shapes=scratch,
        compiler_params=pltpu.CompilerParams(
            collective_id=0, has_side_effects=True, vmem_limit_bytes=40 * 1024 * 1024
        ),
        name="mean_field_backward",
    )(unary_score, affinity, cotangent, compatibility, kernel_weights)
    return grad_unary, grad_affinity, grad_compat, grad_kernel.reshape(NEIGH)


def solution(mesh):
    size_gx, size_gy = mesh.shape["gx"], mesh.shape["gy"]
    size_near = 4 if size_gy % 4 == 0 else 1
    sizes = (size_gx, size_gy, size_gy // size_near, size_near)
    in_specs = (P("gx", "gy", None), P("gx", "gy", None), P(), P(), P("gx", "gy", None))
    out_specs = (P("gx", "gy", None), P("gx", "gy", None), P(), P())
    return jax.shard_map(
        functools.partial(shards, sizes),
        mesh=mesh,
        in_specs=in_specs,
        out_specs=out_specs,
        check_vma=False,
    )
```

profile of v0, /device:TPU:1, one launch (start us, length us, event | category | flops | bytes accessed | tf_op | source)
XLA Modules:
  0.0 54.3 jit_solution(6584290617721181039)
XLA Ops:
  0.6 0.0 copy-start
  0.6 0.9 %copy-done = bf16[4,8,1664]{2,1,0:T(8,128)(2,1)S(1)} copy-done((bf16[4,8,1664]{2,1,0:T(8,128)(2,1)S(1)}, bf16[4,8,1664]{2,1,0:T(8,128)(2,1)}, u32[]{:S(2)}) %copy-start) | copy-done | bytes 106520
  1.5 0.0 copy-start.1
  1.5 0.8 %copy-done.1 = bf16[4,8,512]{2,1,0:T(8,128)(2,1)S(1)} copy-done((bf16[4,8,512]{2,1,0:T(8,128)(2,1)S(1)}, bf16[4,8,512]{2,1,0:T(8,128)(2,1)}, u32[]{:S(2)}) %copy-start.1) | copy-done | bytes 32792
  2.3 0.0 copy-start.2
  2.3 0.8 %copy-done.2 = bf16[4,8,512]{2,1,0:T(8,128)(2,1)S(1)} copy-done((bf16[4,8,512]{2,1,0:T(8,128)(2,1)S(1)}, bf16[4,8,512]{2,1,0:T(8,128)(2,1)}, u32[]{:S(2)}) %copy-start.2) | copy-done | bytes 32792
  3.0 0.0 copy-start.3
  3.0 0.7 %copy-done.3 = f32[8,8]{1,0:T(8,128)S(1)} copy-done((f32[8,8]{1,0:T(8,128)S(1)}, f32[8,8]{1,0:T(8,128)}, u32[]{:S(2)}) %copy-start.3) | copy-done | bytes 280
  3.7 0.0 copy-start.4
  3.7 0.7 %copy-done.4 = f32[26]{0:T(128)S(1)} copy-done((f32[26]{0:T(128)S(1)}, f32[26]{0:T(128)}, u32[]{:S(2)}) %copy-start.4) | copy-done | bytes 128
  4.4 47.5 %mean_field_backward.1 = (bf16[4,8,512]{2,1,0:T(8,128)(2,1)S(1)}, bf16[4,8,1664]{2,1,0:T(8,128)(2,1)S(1)}, f32[8,8]{1,0:T(8,128)S(1)}, f32[1,26]{1,0:T(1,128)S(1)}) custom-call(bf16[4,8,512]{2,1,0:T(8,128)(2,1)S(1)} %copy-done.1, bf16[4,8,1664]{2,1,0:T(8,128)(2,1)S(1)} %copy-done, bf16[4,8,512]{2,1,0:T(8,128)(2,1)S(1)} %copy-done.2, f32[8,8]{1,0:T(8,128)S(1)} %copy-done.3, ...), custom_call_target="tpu_custom_call" | custom-call | tf_op jit(solution)/shard_map/mean_field_backward/pallas_call | solution.py:665
  51.9 0.6 %copy.13 = bf16[4,8,512]{2,1,0:T(8,128)(2,1)} copy(bf16[4,8,512]{2,1,0:T(8,128)(2,1)S(1)} %get-tuple-element.16) | data formatting | bytes 65536
  52.5 0.6 %copy.14 = bf16[4,8,1664]{2,1,0:T(8,128)(2,1)} copy(bf16[4,8,1664]{2,1,0:T(8,128)(2,1)S(1)} %get-tuple-element.17) | data formatting | bytes 212992
  53.2 0.6 %copy.15 = f32[8,8]{1,0:T(8,128)} copy(f32[8,8]{1,0:T(8,128)S(1)} %get-tuple-element.18) | data formatting | bytes 512
  53.7 0.5 copy.16
Async XLA Ops:
  0.6 0.9 %copy-start = (bf16[4,8,1664]{2,1,0:T(8,128)(2,1)S(1)}, bf16[4,8,1664]{2,1,0:T(8,128)(2,1)}, u32[]{:S(2)}) copy-start(bf16[4,8,1664]{2,1,0:T(8,128)(2,1)} %affinity_hbm.1) | copy-start | bytes 319492
  1.5 0.8 %copy-start.1 = (bf16[4,8,512]{2,1,0:T(8,128)(2,1)S(1)}, bf16[4,8,512]{2,1,0:T(8,128)(2,1)}, u32[]{:S(2)}) copy-start(bf16[4,8,512]{2,1,0:T(8,128)(2,1)} %unary_hbm.1) | copy-start | bytes 98308
  2.3 0.8 %copy-start.2 = (bf16[4,8,512]{2,1,0:T(8,128)(2,1)S(1)}, bf16[4,8,512]{2,1,0:T(8,128)(2,1)}, u32[]{:S(2)}) copy-start(bf16[4,8,512]{2,1,0:T(8,128)(2,1)} %cotangent_hbm.1) | copy-start | bytes 98308
  3.0 0.7 %copy-start.3 = (f32[8,8]{1,0:T(8,128)S(1)}, f32[8,8]{1,0:T(8,128)}, u32[]{:S(2)}) copy-start(f32[8,8]{1,0:T(8,128)} %compat.1) | copy-start | bytes 772
  3.7 0.7 %copy-start.4 = (f32[26]{0:T(128)S(1)}, f32[26]{0:T(128)}, u32[]{:S(2)}) copy-start(f32[26]{0:T(128)} %strength.1) | copy-start | bytes 316
where the time goes:
time: 55.2 us; the launch traced here: 54.3 us
  Pallas kernels  47.5 us (86%)
  local copies, waits for them, and re-layouts  6.11 us (11%)
  between operations  0.65 us (1%)
    pallas_call x1, Pallas kernels, shards(): pl.pallas_call(functools.partial(kernel, sizes), out_shape=(jax.ShapeDtyp...  47.5 us
    unnamed x14, local copies, waits for them, and re-layouts  6.11 us

commit v1 on v0

--- a/solution.py
+++ b/solution.py
@@ -25,8 +25,9 @@
 SPAN = 12
 TALL = 24
 BASE = 8
-DIRECTIONS = [(-1, 0), (1, 0), (0, -1), (0, 1), (-1, -1), (-1, 1), (1, -1), (1, 1)]
+DIRECTIONS = [(-1, -1), (-1, 1), (1, -1), (1, 1), (0, -1), (0, 1), (-1, 0), (1, 0)]
 WIDE = 32
+GRANT = 64 * 1024 * 1024 - 65536
 MESH = pl.DeviceIdType.MESH
 
 
@@ -139,8 +140,8 @@
     unary_hbm,
     affinity_hbm,
     cotangent_hbm,
-    compat,
-    strength,
+    compat_hbm,
+    strength_hbm,
     grad_unary_hbm,
     grad_affinity_hbm,
     grad_compat,
@@ -150,6 +151,8 @@
     cotangent_in,
     unary_out,
     affinity_out,
+    compat,
+    strength,
     inner_u,
     sides_u,
     minus_u,
@@ -195,7 +198,7 @@
     total_r,
     gather_a,
     gather_b,
-    gather_c,
+    last,
     load_sem,
     store_sem,
     halo_send,
@@ -206,6 +209,8 @@
     size_gx, size_gy, size_far, size_near = sizes
     me_x, me_y = lax.axis_index("gx"), lax.axis_index("gy")
     me_far, me_near = me_y // size_near, lax.rem(me_y, size_near)
+    chips = size_gx // 2
+    chip, core = me_x // 2, lax.rem(me_x, 2)
     low = low_half()
 
     def around(index, step, size):
@@ -215,6 +220,8 @@
         pltpu.make_async_copy(unary_hbm, unary_in, load_sem.at[0]),
         pltpu.make_async_copy(affinity_hbm, affinity_in, load_sem.at[1]),
         pltpu.make_async_copy(cotangent_hbm, cotangent_in, load_sem.at[2]),
+        pltpu.make_async_copy(strength_hbm, strength, load_sem.at[3]),
+        pltpu.make_async_copy(compat_hbm, compat, load_sem.at[4]),
     ]
     for load in loads:
         load.start()
@@ -223,19 +230,34 @@
         (around(me_x, step_x, size_gx), around(me_y, step_y, size_gy))
         for step_x, step_y in DIRECTIONS
     ]
-    peers_a = [(around(me_x, step, size_gx), me_y) for step in range(1, size_gx)]
+    partner = (me_x + 1 - 2 * core, me_y)
+    odd = [(2 * around(chip, step, chips) + 1, me_y) for step in range(chips)]
+    even = [(2 * around(chip, step, chips), me_y) for step in range(chips)]
+
+    def ring(step, size):
+        return min(step, size - step)
+
+    hops = sorted(
+        [(far, near) for far in range(size_far) for near in range(size_near)][1:],
+        key=lambda hop: -ring(hop[0], size_far) - ring(hop[1], size_near),
+    )
     peers_b = [
-        (me_x, around(me_far, step, size_far) * size_near + me_near)
-        for step in range(1, size_far)
+        (me_x, around(me_far, far, size_far) * size_near + around(me_near, near, size_near))
+        for far, near in hops
     ]
-    peers_c = [
-        (me_x, me_far * size_near + around(me_near, step, size_near))
-        for step in range(1, size_near)
-    ]
-    everyone = neighbours + peers_a + peers_b + peers_c
     barrier = pltpu.get_barrier_semaphore()
-    for device in everyone:
-        pl.semaphore_signal(barrier, inc=1, device_id=device, device_id_type=MESH)
+
+    def greet(devices):
+        for device in devices:
+            pl.semaphore_signal(barrier, inc=1, device_id=device, device_id_type=MESH)
+
+    greet(neighbours + [partner])
+
+    @pl.when(core == 1)
+    def _():
+        greet(odd[1:] + even[1:] + peers_b)
+
+    heard = len(neighbours) + jnp.where(core == 1, chips + len(peers_b), chips)
 
     def exchange(number, width, reach, inner, sides, minus, plus):
         copies = []
@@ -299,10 +321,10 @@
             lay_out(inner_u, sides_u, LABELS, label, held[(label, 0)], value)
 
     spread(unary_in, 4, keep)
-    pl.semaphore_wait(barrier, len(everyone))
-    sent_u = exchange(0, LABELS, 1, inner_u, sides_u, minus_u, plus_u)
 
     loads[1].wait()
+    loads[3].wait()
+    loads[4].wait()
     mask_own_y = {step: mask_y(step) for step in (-1, 0, 1)}
 
     def keep_affinity(number, p, value):
@@ -321,6 +343,8 @@
     inner_send[0:edge, :] = inner_a[edge : 2 * edge, :].astype(jnp.bfloat16)
     inner_send[edge : 2 * edge, :] = inner_a[4 * edge : 5 * edge, :].astype(jnp.bfloat16)
     sides_send[...] = sides_a[...].astype(jnp.bfloat16)
+    pl.semaphore_wait(barrier, heard)
+    sent_u = exchange(0, LABELS, 1, inner_u, sides_u, minus_u, plus_u)
     copies_a = []
     for d, (step_x, step_y) in enumerate(DIRECTIONS):
         if step_x == 0:
@@ -503,7 +527,7 @@
     local = jnp.zeros((8, 128), jnp.float32)
     for b in range(LABELS):
         total = jnp.sum(jnp.sum(total_c[b], axis=1), axis=1, keepdims=True)
-        local = jnp.where(lane == b, total, local)
+        local = jnp.where(lane == 8 * b + sublane, total, local)
     joint_rows = []
     for number, (step_x, step_y, step_z) in enumerate(OFFSETS):
         row = None
@@ -518,33 +542,27 @@
         rows = joint_rows[8 * group : 8 * (group + 1)]
         rows = rows + [jnp.zeros((1, 128), jnp.float32)] * (8 - len(rows))
         total = jnp.sum(jnp.concatenate(rows, axis=0), axis=1, keepdims=True)
-        local = jnp.where(lane == LABELS + group, total, local)
-
-    def share(buffer, me, peers, base, value):
-        buffer[me] = value
-        copies = [
-            pltpu.make_async_remote_copy(
-                src_ref=buffer.at[me],
-                dst_ref=buffer.at[me],
-                send_sem=peer_send.at[base + place],
-                recv_sem=peer_recv.at[base + place],
-                device_id=device,
-                device_id_type=MESH,
-            )
-            for place, device in enumerate(peers)
-        ]
-        for copy in copies:
-            copy.start()
-        return copies
-
-    def collect(buffer, copies):
-        arrive(copies)
-        total = buffer[0]
-        for place in range(1, buffer.shape[0]):
-            total = total + buffer[place]
-        return total
-
-    shared_a = share(gather_a, me_x, peers_a, 0, local)
+        local = jnp.where(lane == 8 * (LABELS + group) + sublane, total, local)
+
+    gather_a[me_x] = jnp.sum(local, axis=0, keepdims=True)
+
+    def to_peer(buffer, me, place_send, place_recv, device):
+        return pltpu.make_async_remote_copy(
+            src_ref=buffer.at[me],
+            dst_ref=buffer.at[me],
+            send_sem=peer_send.at[place_send],
+            recv_sem=peer_recv.at[place_recv],
+            device_id=device,
+            device_id_type=MESH,
+        )
+
+    along_x = [to_peer(gather_a, me_x, step, 2 * step + core, odd[step]) for step in range(chips)]
+    for step in sorted(range(1, chips), key=lambda step: -ring(step, chips)):
+        along_x[step].start()
+
+    @pl.when(core == 0)
+    def _():
+        along_x[0].start()
 
     def put_affinity(tile, x, value):
         affinity_out[x, :, 128 * tile : 128 * (tile + 1)] = value.astype(jnp.bfloat16)
@@ -559,7 +577,6 @@
             found = assemble(inner_h, minus_h, plus_h, LABELS, label, y, 1)
             for p in (-1, 0, 1, 2):
                 put_field(field_i, label, p, y, found[p])
-    shared_b = share(gather_b, me_far, peers_b, len(peers_a), collect(gather_a, shared_a))
     sums = message(back_weight_at(0), field_i, (0, 1), 0)
     for p in (0, 1):
         current = field_0[1, :, p + 2, pl.ds(BASE, 8), :]
@@ -572,22 +589,73 @@
     store_u = pltpu.make_async_copy(unary_out, grad_unary_hbm, store_sem.at[1])
     store_u.start()
 
-    shared_c = share(
-        gather_c, me_near, peers_c, len(peers_a) + len(peers_b), collect(gather_b, shared_b)
-    )
+    base = 2 * chips
+    along_y = [
+        to_peer(gather_b, me_y, base + place, base + place, device)
+        for place, device in enumerate(peers_b)
+    ]
+    to_even = to_peer(last, 0, base + len(peers_b), base + len(peers_b), partner)
+
+    @pl.when(core == 1)
+    def _():
+        for step in range(chips):
+            for sender in (0, 1):
+                if (step, sender) != (0, 1):
+                    to_peer(gather_a, me_x, 0, 2 * step + sender, partner).wait_recv()
+        total = gather_a[0]
+        for place in range(1, size_gx):
+            total = total + gather_a[place]
+        gather_b[me_y] = total
+        for copy in along_y:
+            copy.start()
+        for copy in along_y:
+            copy.wait_recv()
+        total = gather_b[0]
+        for place in range(1, size_gy):
+            total = total + gather_b[place]
+        last[0] = total
+        to_even.start()
+
+    @pl.when(core == 0)
+    def _():
+        to_even.wait_recv()
+
     voxels = size_gx * 4 * size_gy * 8 * DEPTH
-    final = collect(gather_c, shared_c) * (1.0 / math.sqrt(voxels))
-    grad_compat[...] = final[:, :LABELS]
-    picked = jnp.zeros((8, 128), jnp.float32)
-    for group in range(4):
-        wanted = lane == 8 * group + sublane
-        picked = jnp.where(wanted, final[:, LABELS + group : LABELS + group + 1], picked)
-    grad_kernel[...] = jnp.sum(picked, axis=0, keepdims=True)[:, :NEIGH]
-
-    for copy in sent_u + copies_a + sent_q + sent_g + sent_h + shared_a + shared_b + shared_c:
+    final = last[0] * (1.0 / math.sqrt(voxels))
+    grad_kernel[...] = pltpu.roll(final, 128 - LABELS * LABELS, 1)[:, :NEIGH]
+    spaced = jnp.where(lax.rem(lane, 8) == sublane, jnp.broadcast_to(final, (8, 128)), 0.0)
+    table = jnp.zeros((8, 128), jnp.float32)
+    for b in range(LABELS):
+        column = jnp.sum(jnp.where(lane // 8 == b, spaced, 0.0), axis=1, keepdims=True)
+        table = jnp.where(lane == b, column, table)
+    grad_compat[...] = table[:, :LABELS]
+
+    for copy in sent_u + copies_a + sent_q + sent_g + sent_h + along_x[1:]:
         copy.wait_send()
+
+    @pl.when(core == 0)
+    def _():
+        along_x[0].wait_send()
+
+    @pl.when(core == 1)
+    def _():
+        for copy in along_y + [to_even]:
+            copy.wait_send()
+
     store_a.wait()
     store_u.wait()
+
+
+def hand_out(*refs):
+    parts, results, sem = refs[:4], refs[4:8], refs[8]
+    copies = [
+        pltpu.make_async_copy(part, result, sem.at[number])
+        for number, (part, result) in enumerate(zip(parts, results))
+    ]
+    for copy in copies:
+        copy.start()
+    for copy in copies:
+        copy.wait()
 
 
 def shards(sizes, unary_score, affinity, compatibility, kernel_weights, cotangent):
@@ -608,7 +676,7 @@
     field = pltpu.VMEM((3, LABELS, 6, TALL, 128), f32)
     pair = pltpu.VMEM((LABELS, 2, 8, 128), f32)
     rim = pltpu.VMEM((LABELS, 4, TALL, 128), f32)
-    peers = size_gx + size_far + size_near - 3
+    peers = size_gx + size_gy
     scratch = (
         [
             pltpu.VMEM(unary_score.shape, bf16),
@@ -616,6 +684,8 @@
             pltpu.VMEM(cotangent.shape, bf16),
             pltpu.VMEM(unary_score.shape, bf16),
             pltpu.VMEM(affinity.shape, bf16),
+            pltpu.SMEM(compatibility.shape, f32),
+            pltpu.SMEM(kernel_weights.shape, f32),
         ]
         + exchanged(LABELS)
         + exchanged(WIDE)
@@ -648,10 +718,10 @@
             pair,
             pltpu.VMEM((LABELS, LABELS, 8, 128), f32),
             pltpu.VMEM((NEIGH, 2, 8, 128), f32),
-            pltpu.VMEM((size_gx, 8, 128), f32),
-            pltpu.VMEM((size_far, 8, 128), f32),
-            pltpu.VMEM((size_near, 8, 128), f32),
-            pltpu.SemaphoreType.DMA((3,)),
+            pltpu.VMEM((size_gx, 1, 128), f32),
+            pltpu.VMEM((size_gy, 1, 128), f32),
+            pltpu.VMEM((1, 1, 128), f32),
+            pltpu.SemaphoreType.DMA((5,)),
             pltpu.SemaphoreType.DMA((2,)),
             pltpu.SemaphoreType.DMA((5, 8)),
             pltpu.SemaphoreType.DMA((5, 8)),
@@ -660,7 +730,7 @@
         ]
     )
     anywhere = pl.BlockSpec(memory_space=pl.ANY)
-    scalars = pl.BlockSpec(memory_space=pltpu.SMEM)
+    in_hbm = pl.BlockSpec(memory_space=pltpu.HBM)
     vectors = pl.BlockSpec(memory_space=pltpu.VMEM)
     grad_unary, grad_affinity, grad_compat, grad_kernel = pl.pallas_call(
         functools.partial(kernel, sizes),
@@ -670,15 +740,24 @@
             jax.ShapeDtypeStruct((LABELS, LABELS), f32),
             jax.ShapeDtypeStruct((1, NEIGH), f32),
         ),
-        in_specs=[anywhere, anywhere, anywhere, scalars, scalars],
+        in_specs=[in_hbm] * 5,
         out_specs=(anywhere, anywhere, vectors, vectors),
         scratch_shapes=scratch,
         compiler_params=pltpu.CompilerParams(
-            collective_id=0, has_side_effects=True, vmem_limit_bytes=40 * 1024 * 1024
+            collective_id=0, has_side_effects=True, vmem_limit_bytes=GRANT
         ),
         name="mean_field_backward",
     )(unary_score, affinity, cotangent, compatibility, kernel_weights)
-    return grad_unary, grad_affinity, grad_compat, grad_kernel.reshape(NEIGH)
+    found = (grad_unary, grad_affinity, grad_compat, grad_kernel.reshape(NEIGH))
+    return pl.pallas_call(
+        hand_out,
+        out_shape=tuple(jax.ShapeDtypeStruct(part.shape, part.dtype) for part in found),
+        in_specs=[anywhere] * 4,
+        out_specs=(in_hbm,) * 4,
+        scratch_shapes=[pltpu.SemaphoreType.DMA((4,))],
+        compiler_params=pltpu.CompilerParams(vmem_limit_bytes=GRANT),
+        name="hand_out",
+    )(*found)
 
 
 def solution(mesh):

time: 55.2 us -> 52.2 us (0.946); the launches traced: 54.3 us -> 52.1 us
  local copies, waits for them, and re-layouts: 6.11 us -> 0 us
  Pallas kernels: 47.5 us -> 51.5 us
    unnamed x14 -> x0, local copies, waits for them, and re-layouts: 6.11 us -> none
    pallas_call x0 -> x1, Pallas kernels: none -> 5.5 us  [shards(): pl.pallas_call(hand_out, out_shape=tuple((jax.ShapeDtypeStruct(part.shape...]
    pallas_call x1, Pallas kernels: 47.5 us -> 46 us  [shards(): pl.pallas_call(functools.partial(kernel, sizes), out_shape=(jax.ShapeDtyp...]
where the time goes in v1:
time: 52.2 us; the launch traced here: 52.1 us
  Pallas kernels  51.5 us (99%)
  between operations  0.64 us (1%)
    pallas_call x1, Pallas kernels, shards(): pl.pallas_call(functools.partial(kernel, sizes), out_shape=(jax.ShapeDtyp...  46 us
    pallas_call x1, Pallas kernels, shards(): pl.pallas_call(hand_out, out_shape=tuple((jax.ShapeDtypeStruct(part.shape...  5.5 us

profile of v1, /device:TPU:1, one launch (start us, length us, event | category | flops | bytes accessed | tf_op | source)
XLA Modules:
  0.0 52.1 jit_solution(12493736511033627536)
XLA Ops:
  0.6 46.0 %mean_field_backward.1 = (bf16[4,8,512]{2,1,0:T(8,128)(2,1)}, bf16[4,8,1664]{2,1,0:T(8,128)(2,1)}, f32[8,8]{1,0:T(8,128)}, f32[1,26]{1,0:T(1,128)}) custom-call(bf16[4,8,512]{2,1,0:T(8,128)(2,1)} %unary_hbm.1, bf16[4,8,1664]{2,1,0:T(8,128)(2,1)} %affinity_hbm.1, bf16[4,8,512]{2,1,0:T(8,128)(2,1)} %cotangent_hbm.1, f32[8,8]{1,0:T(8,128)} %compat_hbm.1, ...), custom_call_target="tpu_custom_call" | custom-call | tf_op jit(solution)/shard_map/mean_field_backward/pallas_call | solution.py:735
  46.6 5.5 %hand_out.1 = (bf16[4,8,512]{2,1,0:T(8,128)(2,1)}, bf16[4,8,1664]{2,1,0:T(8,128)(2,1)}, f32[8,8]{1,0:T(8,128)}, f32[26]{0:T(128)}) custom-call(bf16[4,8,512]{2,1,0:T(8,128)(2,1)} %get-tuple-element.8.refs_0_, bf16[4,8,1664]{2,1,0:T(8,128)(2,1)} %get-tuple-element.9.refs_1_, f32[8,8]{1,0:T(8,128)} %get-tuple-element.10.refs_2_, f32[26]{0:T(128)} %bitcast.1), custom_call_target="tpu_custom_call" | custom-call | tf_op jit(solution)/shard_map/hand_out/pallas_call | solution.py:752

commit v2 on v1

--- a/solution.py
+++ b/solution.py
@@ -128,11 +128,30 @@
     return current * (grad_in - jnp.sum(current * grad_in, axis=0, keepdims=True))
 
 
-def put_field(field, label, p, y, value):
-    axis = value.ndim - 1
-    field[1, label, p + 2, pl.ds(BASE + y, 8), :] = value
-    field[0, label, p + 2, pl.ds(BASE + y, 8), :] = pltpu.roll(value, 1, axis)
-    field[2, label, p + 2, pl.ds(BASE + y, 8), :] = pltpu.roll(value, 127, axis)
+def put_shifts(field, p, y, values):
+    field[0, :, p + 2, pl.ds(BASE + y, 8), :] = pltpu.roll(values, 1, 2)
+    field[2, :, p + 2, pl.ds(BASE + y, 8), :] = pltpu.roll(values, 127, 2)
+
+
+def put_field(field, p, y, values):
+    field[1, :, p + 2, pl.ds(BASE + y, 8), :] = values
+    put_shifts(field, p, y, values)
+
+
+def rim_tiles(reach):
+    return range(-reach, 2 + reach), (-2, 2) if reach == 2 else (-1, 1)
+
+
+def gather_field(field, inner, minus, plus, reach):
+    columns, starts = rim_tiles(reach)
+    for label in range(LABELS):
+        for y in starts:
+            found = assemble(inner, minus, plus, LABELS, label, y, reach)
+            for p in columns:
+                field[1, label, p + 2, pl.ds(BASE + y, 8), :] = found[p]
+    for y in starts:
+        for p in columns:
+            put_shifts(field, p, y, field[1, :, p + 2, pl.ds(BASE + y, 8), :])
 
 
 def kernel(
@@ -161,51 +180,51 @@
     sides_a,
     minus_a,
     plus_a,
-    inner_send,
-    sides_send,
-    inner_recv,
-    minus_recv,
-    plus_recv,
-    inner_q,
-    sides_q,
-    minus_q,
-    plus_q,
-    inner_g,
-    sides_g,
-    minus_g,
-    plus_g,
-    inner_h,
-    sides_h,
-    minus_h,
-    plus_h,
-    logits,
-    own_grad,
-    field_0,
-    field_1,
-    field_2,
-    field_g,
-    field_h,
-    field_i,
-    wide_aff,
-    weight_own,
-    weight_rim,
-    weight_back,
-    message_1,
-    message_2,
-    rim_p,
-    total_u,
-    total_c,
-    total_r,
-    gather_a,
-    gather_b,
-    last,
-    load_sem,
-    store_sem,
-    halo_send,
-    halo_recv,
-    peer_send,
-    peer_recv,
+    *rest,
 ):
+    boxes, rest = rest[:15], rest[15:]
+    box_u, box_a, box_g = boxes[:5], boxes[5:10], boxes[10:]
+    (
+        inner_q,
+        sides_q,
+        minus_q,
+        plus_q,
+        inner_g,
+        sides_g,
+        minus_g,
+        plus_g,
+        inner_h,
+        sides_h,
+        minus_h,
+        plus_h,
+        logits,
+        own_grad,
+        field_0,
+        field_1,
+        field_2,
+        field_g,
+        field_h,
+        field_i,
+        wide_aff,
+        weight_own,
+        weight_rim,
+        weight_back,
+        message_1,
+        message_2,
+        rim_p,
+        total_u,
+        total_c,
+        total_r,
+        gather_a,
+        gather_b,
+        last,
+        load_sem,
+        store_sem,
+        halo_send,
+        halo_recv,
+        peer_send,
+        peer_recv,
+    ) = rest
     size_gx, size_gy, size_far, size_near = sizes
     me_x, me_y = lax.axis_index("gx"), lax.axis_index("gy")
     me_far, me_near = me_y // size_near, lax.rem(me_y, size_near)
@@ -297,6 +316,49 @@
         for copy in copies:
             copy.wait_recv()
 
+    def narrow(width, reach, inner, sides, box):
+        inner_send, sides_send = box[:2]
+        part = reach * 2 * width
+        for place, first in enumerate((2, 10 - reach)):
+            rows = inner[pl.ds(first * 2 * width, part), :]
+            inner_send[pl.ds(place * part, part), :] = rows.astype(jnp.bfloat16)
+        sides_send[...] = sides[...].astype(jnp.bfloat16)
+
+    def start_narrow(number, reach, box):
+        inner_send, sides_send, inner_recv, minus_recv, plus_recv = box
+        width = sides_send.shape[0] // 16
+        part = reach * 2 * width
+        copies = []
+        for d, (step_x, step_y) in enumerate(DIRECTIONS):
+            if step_x == 0:
+                rows = pl.ds(0 if step_y < 0 else part, part)
+                source, target = inner_send.at[rows, :], inner_recv.at[rows, :]
+            else:
+                start = 0 if step_x < 0 else 8 * width
+                landing = plus_recv if step_x < 0 else minus_recv
+                if step_y == 0:
+                    source = sides_send.at[pl.ds(start, 8 * width), :]
+                    target = landing.at[pl.ds(2 * width, 8 * width), :]
+                else:
+                    first = 0 if step_y < 0 else 6
+                    land = 10 if step_y < 0 else 0
+                    source = sides_send.at[pl.ds(start + first * width, 2 * width), :]
+                    target = landing.at[pl.ds(land * width, 2 * width), :]
+            copies.append(remote(number, d, source, target))
+        for copy in copies:
+            copy.start()
+        return copies
+
+    def arrive_narrow(copies, width, reach, inner, minus, plus, box):
+        inner_recv, minus_recv, plus_recv = box[2:]
+        part = reach * 2 * width
+        arrive(copies)
+        for place, land in enumerate((10, 2 - reach)):
+            rows = inner_recv[pl.ds(place * part, part), :]
+            inner[pl.ds(land * 2 * width, part), :] = rows.astype(jnp.float32)
+        minus[...] = minus_recv[...].astype(jnp.float32)
+        plus[...] = plus_recv[...].astype(jnp.float32)
+
     lane = lax.broadcasted_iota(jnp.int32, (8, 128), 1)
     depth = lax.rem(lane, DEPTH)
     half = lane // DEPTH
@@ -339,33 +401,13 @@
     nothing = jnp.zeros((8, 128), jnp.float32)
     for number in range(NEIGH, WIDE):
         lay_out(inner_a, sides_a, WIDE, number, nothing, nothing)
-    edge = 2 * 2 * WIDE
-    inner_send[0:edge, :] = inner_a[edge : 2 * edge, :].astype(jnp.bfloat16)
-    inner_send[edge : 2 * edge, :] = inner_a[4 * edge : 5 * edge, :].astype(jnp.bfloat16)
-    sides_send[...] = sides_a[...].astype(jnp.bfloat16)
+    narrow(LABELS, 1, inner_u, sides_u, box_u)
+    narrow(WIDE, 2, inner_a, sides_a, box_a)
     pl.semaphore_wait(barrier, heard)
-    sent_u = exchange(0, LABELS, 1, inner_u, sides_u, minus_u, plus_u)
-    copies_a = []
-    for d, (step_x, step_y) in enumerate(DIRECTIONS):
-        if step_x == 0:
-            part = pl.ds(0 if step_y < 0 else edge, edge)
-            source, target = inner_send.at[part, :], inner_recv.at[part, :]
-        else:
-            start = 0 if step_x < 0 else 8 * WIDE
-            landing = plus_recv if step_x < 0 else minus_recv
-            if step_y == 0:
-                source = sides_send.at[pl.ds(start, 8 * WIDE), :]
-                target = landing.at[pl.ds(2 * WIDE, 8 * WIDE), :]
-            else:
-                first = 0 if step_y < 0 else 6
-                land = 10 if step_y < 0 else 0
-                source = sides_send.at[pl.ds(start + first * WIDE, 2 * WIDE), :]
-                target = landing.at[pl.ds(land * WIDE, 2 * WIDE), :]
-        copies_a.append(remote(1, d, source, target))
-    for copy in copies_a:
-        copy.start()
-
-    arrive(sent_u)
+    sent_u = start_narrow(0, 1, box_u)
+    sent_a = start_narrow(1, 2, box_a)
+
+    arrive_narrow(sent_u, LABELS, 1, inner_u, minus_u, plus_u, box_u)
     for label in range(LABELS):
         for y in (-1, 1):
             found = assemble(inner_u, minus_u, plus_u, LABELS, label, y, 1)
@@ -374,7 +416,7 @@
     for y in (-1, 1):
         for p in (-1, 0, 1, 2):
             value = normalise(logits[:, p + 2, pl.ds(BASE + y, 8), :])
-            put_field(field_0, slice(None), p, y, value)
+            put_field(field_0, p, y, value)
 
     def own_logits(p):
         return logits[:, p + 2, pl.ds(BASE, 8), :]
@@ -388,9 +430,12 @@
     def backward(b, a):
         return compat[a, b]
 
-    def send_field(number, reach, values, inner, sides, minus, plus):
+    def lay_field(values, inner, sides):
         for label in range(LABELS):
             lay_out(inner, sides, LABELS, label, values[0][label], values[1][label])
+
+    def send_field(number, reach, values, inner, sides, minus, plus):
+        lay_field(values, inner, sides)
         return exchange(number, LABELS, reach, inner, sides, minus, plus)
 
     sums = message(own_weight, field_0, (0, 1), 0)
@@ -406,11 +451,7 @@
         own_grad[label, p] = value
 
     spread(cotangent_in, 4, keep_cotangent)
-    arrive(copies_a)
-    inner_a[0:edge, :] = inner_recv[edge : 2 * edge, :].astype(jnp.float32)
-    inner_a[5 * edge : 6 * edge, :] = inner_recv[0:edge, :].astype(jnp.float32)
-    minus_a[...] = minus_recv[...].astype(jnp.float32)
-    plus_a[...] = plus_recv[...].astype(jnp.float32)
+    arrive_narrow(sent_a, WIDE, 2, inner_a, minus_a, plus_a, box_a)
     for number in range(NEIGH):
         for y in (-2, 2):
             found = assemble(inner_a, minus_a, plus_a, WIDE, number, y, 2)
@@ -441,11 +482,7 @@
     rim_weights(weight_rim, rim_value)
 
     arrive(sent_q)
-    for label in range(LABELS):
-        for y in (-2, 2):
-            found = assemble(inner_q, minus_q, plus_q, LABELS, label, y, 2)
-            for p in range(-2, 4):
-                put_field(field_1, label, p, y, found[p])
+    gather_field(field_1, inner_q, minus_q, plus_q, 2)
     for y in (-1, 1):
 
         def rim_weight(number, p, y=y):
@@ -455,7 +492,7 @@
         for p in (-1, 0, 1, 2):
             message_2[:, p + 1, pl.ds(BASE + y, 8), :] = sums[p]
             here = logits[:, p + 2, pl.ds(BASE + y, 8), :]
-            put_field(field_2, slice(None), p, y, normalise(here - mix(forward, sums[p])))
+            put_field(field_2, p, y, normalise(here - mix(forward, sums[p])))
 
     sums = message(own_weight, field_2, (0, 1), 0)
     grads = []
@@ -466,7 +503,9 @@
         total_u[:, p] = step
         grads.append(-step)
         values.append(mix(backward, -step))
-    sent_g = send_field(3, 2, values, inner_g, sides_g, minus_g, plus_g)
+    lay_field(values, inner_g, sides_g)
+    narrow(LABELS, 2, inner_g, sides_g, box_g)
+    sent_g = start_narrow(3, 2, box_g)
 
     def add_compat(grads, messages, begin):
         for b in range(LABELS):
@@ -484,12 +523,8 @@
     add_kernel(values, field_2, True)
     rim_weights(weight_back, back_value)
 
-    arrive(sent_g)
-    for label in range(LABELS):
-        for y in (-2, 2):
-            found = assemble(inner_g, minus_g, plus_g, LABELS, label, y, 2)
-            for p in range(-2, 4):
-                put_field(field_g, label, p, y, found[p])
+    arrive_narrow(sent_g, LABELS, 2, inner_g, minus_g, plus_g, box_g)
+    gather_field(field_g, inner_g, minus_g, plus_g, 2)
 
     def back_weight_at(y):
         def back_weight(number, p):
@@ -503,7 +538,7 @@
             current = field_2[1, :, p + 2, pl.ds(BASE + y, 8), :]
             grad_p = -softmax_back(current, sums[p])
             rim_p[:, p + 1, pl.ds(BASE + y, 8), :] = grad_p
-            put_field(field_h, slice(None), p, y, mix(backward, grad_p))
+            put_field(field_h, p, y, mix(backward, grad_p))
 
     sums = message(back_weight_at(0), field_h, (0, 1), 0)
     grads_1 = []
@@ -572,11 +607,7 @@
     store_a.start()
 
     arrive(sent_h)
-    for label in range(LABELS):
-        for y in (-1, 1):
-            found = assemble(inner_h, minus_h, plus_h, LABELS, label, y, 1)
-            for p in (-1, 0, 1, 2):
-                put_field(field_i, label, p, y, found[p])
+    gather_field(field_i, inner_h, minus_h, plus_h, 1)
     sums = message(back_weight_at(0), field_i, (0, 1), 0)
     for p in (0, 1):
         current = field_0[1, :, p + 2, pl.ds(BASE, 8), :]
@@ -630,7 +661,7 @@
         table = jnp.where(lane == b, column, table)
     grad_compat[...] = table[:, :LABELS]
 
-    for copy in sent_u + copies_a + sent_q + sent_g + sent_h + along_x[1:]:
+    for copy in sent_u + sent_a + sent_q + sent_g + sent_h + along_x[1:]:
         copy.wait_send()
 
     @pl.when(core == 0)
@@ -647,14 +678,21 @@
 
 
 def hand_out(*refs):
-    parts, results, sem = refs[:4], refs[4:8], refs[8]
-    copies = [
-        pltpu.make_async_copy(part, result, sem.at[number])
-        for number, (part, result) in enumerate(zip(parts, results))
+    parts, results, held, sem = refs[:4], refs[4:8], refs[8:12], refs[12]
+    inward = [
+        pltpu.make_async_copy(part, hold, sem.at[0, number])
+        for number, (part, hold) in enumerate(zip(parts, held))
     ]
-    for copy in copies:
+    outward = [
+        pltpu.make_async_copy(hold, result, sem.at[1, number])
+        for number, (hold, result) in enumerate(zip(held, results))
+    ]
+    for copy in inward:
         copy.start()
-    for copy in copies:
+    for came, copy in zip(inward, outward):
+        came.wait()
+        copy.start()
+    for copy in outward:
         copy.wait()
 
 
@@ -671,6 +709,15 @@
             rows(2 * 8 * width),
             rows(SPAN * width),
             rows(SPAN * width),
+        ]
+
+    def boxed(width, reach):
+        return [
+            rows(2 * reach * 2 * width, bf16),
+            rows(2 * 8 * width, bf16),
+            rows(2 * reach * 2 * width, bf16),
+            rows(SPAN * width, bf16),
+            rows(SPAN * width, bf16),
         ]
 
     field = pltpu.VMEM((3, LABELS, 6, TALL, 128), f32)
@@ -689,13 +736,9 @@
         ]
         + exchanged(LABELS)
         + exchanged(WIDE)
-        + [
-            rows(2 * 4 * WIDE, bf16),
-            rows(2 * 8 * WIDE, bf16),
-            rows(2 * 4 * WIDE, bf16),
-            rows(SPAN * WIDE, bf16),
-            rows(SPAN * WIDE, bf16),
-        ]
+        + boxed(LABELS, 1)
+        + boxed(WIDE, 2)
+        + boxed(LABELS, 2)
         + exchanged(LABELS)
         + exchanged(LABELS)
         + exchanged(LABELS)
@@ -754,7 +797,8 @@
         out_shape=tuple(jax.ShapeDtypeStruct(part.shape, part.dtype) for part in found),
         in_specs=[anywhere] * 4,
         out_specs=(in_hbm,) * 4,
-        scratch_shapes=[pltpu.SemaphoreType.DMA((4,))],
+        scratch_shapes=[pltpu.VMEM(part.shape, part.dtype) for part in found]
+        + [pltpu.SemaphoreType.DMA((2, 4))],
         compiler_params=pltpu.CompilerParams(vmem_limit_bytes=GRANT),
         name="hand_out",
     )(*found)

time: 52.2 us -> 48.3 us (0.925)
  Pallas kernels: 51.5 us -> 47.5 us
    pallas_call x1, Pallas kernels: 5.5 us -> 1.63 us  [shards(): pl.pallas_call(hand_out, out_shape=tuple((jax.ShapeDtypeStruct(part.shape...]
where the time goes in v2:
time: 48.3 us; the launch traced here: 48.2 us
  Pallas kernels  47.5 us (98%)
  between operations  0.64 us (1%)
    pallas_call x1, Pallas kernels, shards(): pl.pallas_call(functools.partial(kernel, sizes), out_shape=(jax.ShapeDtyp...  45.9 us
    pallas_call x1, Pallas kernels, shards(): pl.pallas_call(hand_out, out_shape=tuple((jax.ShapeDtypeStruct(part.shape...  1.63 us

profile of v2, /device:TPU:1, one launch (start us, length us, event | category | flops | bytes accessed | tf_op | source)
XLA Modules:
  0.0 48.2 jit_solution(5358018640619418935)
XLA Ops:
  0.6 45.9 %mean_field_backward.1 = (bf16[4,8,512]{2,1,0:T(8,128)(2,1)}, bf16[4,8,1664]{2,1,0:T(8,128)(2,1)}, f32[8,8]{1,0:T(8,128)}, f32[1,26]{1,0:T(1,128)}) custom-call(bf16[4,8,512]{2,1,0:T(8,128)(2,1)} %unary_hbm.1, bf16[4,8,1664]{2,1,0:T(8,128)(2,1)} %affinity_hbm.1, bf16[4,8,512]{2,1,0:T(8,128)(2,1)} %cotangent_hbm.1, f32[8,8]{1,0:T(8,128)} %compat_hbm.1, ...), custom_call_target="tpu_custom_call" | custom-call | tf_op jit(solution)/shard_map/mean_field_backward/pallas_call | solution.py:778
  46.5 1.6 %hand_out.1 = (bf16[4,8,512]{2,1,0:T(8,128)(2,1)}, bf16[4,8,1664]{2,1,0:T(8,128)(2,1)}, f32[8,8]{1,0:T(8,128)}, f32[26]{0:T(128)}) custom-call(bf16[4,8,512]{2,1,0:T(8,128)(2,1)} %get-tuple-element.8.refs_0_, bf16[4,8,1664]{2,1,0:T(8,128)(2,1)} %get-tuple-element.9.refs_1_, f32[8,8]{1,0:T(8,128)} %get-tuple-element.10.refs_2_, f32[26]{0:T(128)} %bitcast.1), custom_call_target="tpu_custom_call" | custom-call | tf_op jit(solution)/shard_map/hand_out/pallas_call | solution.py:795

commit v3 on v2

--- a/solution.py
+++ b/solution.py
@@ -224,6 +224,7 @@
         halo_recv,
         peer_send,
         peer_recv,
+        meet_sem,
     ) = rest
     size_gx, size_gy, size_far, size_near = sizes
     me_x, me_y = lax.axis_index("gx"), lax.axis_index("gy")
@@ -270,13 +271,26 @@
         for device in devices:
             pl.semaphore_signal(barrier, inc=1, device_id=device, device_id_type=MESH)
 
-    greet(neighbours + [partner])
-
-    @pl.when(core == 1)
-    def _():
-        greet(odd[1:] + even[1:] + peers_b)
-
-    heard = len(neighbours) + jnp.where(core == 1, chips + len(peers_b), chips)
+    greet(neighbours)
+
+    rounds = [doubling(size_gx), doubling(size_gy)]
+
+    def meet(stage):
+        for axis in (0, 1):
+            if 0 < stage <= len(rounds[axis]):
+                pl.semaphore_wait(meet_sem.at[axis, stage - 1], 2)
+        for axis in (0, 1):
+            if stage < len(rounds[axis]):
+                step = rounds[axis][stage]
+                for by in (-step, step):
+                    device = (
+                        (around(me_x, by, size_gx), me_y)
+                        if axis == 0
+                        else (me_x, around(me_y, by, size_gy))
+                    )
+                    pl.semaphore_signal(
+                        meet_sem.at[axis, stage], inc=1, device_id=device, device_id_type=MESH
+                    )
 
     def exchange(number, width, reach, inner, sides, minus, plus):
         copies = []
@@ -403,11 +417,13 @@
         lay_out(inner_a, sides_a, WIDE, number, nothing, nothing)
     narrow(LABELS, 1, inner_u, sides_u, box_u)
     narrow(WIDE, 2, inner_a, sides_a, box_a)
-    pl.semaphore_wait(barrier, heard)
+    pl.semaphore_wait(barrier, len(neighbours))
+    meet(0)
     sent_u = start_narrow(0, 1, box_u)
     sent_a = start_narrow(1, 2, box_a)
 
     arrive_narrow(sent_u, LABELS, 1, inner_u, minus_u, plus_u, box_u)
+    meet(1)
     for label in range(LABELS):
         for y in (-1, 1):
             found = assemble(inner_u, minus_u, plus_u, LABELS, label, y, 1)
@@ -482,6 +498,7 @@
     rim_weights(weight_rim, rim_value)
 
     arrive(sent_q)
+    meet(2)
     gather_field(field_1, inner_q, minus_q, plus_q, 2)
     for y in (-1, 1):
 
@@ -524,6 +541,7 @@
     rim_weights(weight_back, back_value)
 
     arrive_narrow(sent_g, LABELS, 2, inner_g, minus_g, plus_g, box_g)
+    meet(3)
     gather_field(field_g, inner_g, minus_g, plus_g, 2)
 
     def back_weight_at(y):
@@ -607,6 +625,7 @@
     store_a.start()
 
     arrive(sent_h)
+    meet(4)
     gather_field(field_i, inner_h, minus_h, plus_h, 1)
     sums = message(back_weight_at(0), field_i, (0, 1), 0)
     for p in (0, 1):
@@ -675,6 +694,14 @@
 
     store_a.wait()
     store_u.wait()
+
+
+def doubling(size):
+    steps, reach = [], 1
+    while reach < size // 2:
+        steps.append(reach)
+        reach *= 2
+    return steps
 
 
 def hand_out(*refs):
@@ -770,6 +797,7 @@
             pltpu.SemaphoreType.DMA((5, 8)),
             pltpu.SemaphoreType.DMA((peers,)),
             pltpu.SemaphoreType.DMA((peers,)),
+            pltpu.SemaphoreType.REGULAR((2, 4)),
         ]
     )
     anywhere = pl.BlockSpec(memory_space=pl.ANY)

time: 48.3 us -> 47.6 us (0.986)
  Pallas kernels: 47.5 us -> 46.7 us
    pallas_call x1, Pallas kernels: 45.9 us -> 45.1 us  [shards(): pl.pallas_call(functools.partial(kernel, sizes), out_shape=(jax.ShapeDtyp...]
where the time goes in v3:
time: 47.6 us; the launch traced here: 47.4 us
  Pallas kernels  46.7 us (98%)
  between operations  0.64 us (1%)
    pallas_call x1, Pallas kernels, shards(): pl.pallas_call(functools.partial(kernel, sizes), out_shape=(jax.ShapeDtyp...  45.1 us
    pallas_call x1, Pallas kernels, shards(): pl.pallas_call(hand_out, out_shape=tuple((jax.ShapeDtypeStruct(part.shape...  1.63 us

profile of v3, /device:TPU:1, one launch (start us, length us, event | category | flops | bytes accessed | tf_op | source)
XLA Modules:
  0.0 47.4 jit_solution(7468642363779651117)
XLA Ops:
  0.6 45.1 %mean_field_backward.1 = (bf16[4,8,512]{2,1,0:T(8,128)(2,1)}, bf16[4,8,1664]{2,1,0:T(8,128)(2,1)}, f32[8,8]{1,0:T(8,128)}, f32[1,26]{1,0:T(1,128)}) custom-call(bf16[4,8,512]{2,1,0:T(8,128)(2,1)} %unary_hbm.1, bf16[4,8,1664]{2,1,0:T(8,128)(2,1)} %affinity_hbm.1, bf16[4,8,512]{2,1,0:T(8,128)(2,1)} %cotangent_hbm.1, f32[8,8]{1,0:T(8,128)} %compat_hbm.1, ...), custom_call_target="tpu_custom_call" | custom-call | tf_op jit(solution)/shard_map/mean_field_backward/pallas_call | solution.py:806
  45.7 1.6 %hand_out.1 = (bf16[4,8,512]{2,1,0:T(8,128)(2,1)}, bf16[4,8,1664]{2,1,0:T(8,128)(2,1)}, f32[8,8]{1,0:T(8,128)}, f32[26]{0:T(128)}) custom-call(bf16[4,8,512]{2,1,0:T(8,128)(2,1)} %get-tuple-element.8.refs_0_, bf16[4,8,1664]{2,1,0:T(8,128)(2,1)} %get-tuple-element.9.refs_1_, f32[8,8]{1,0:T(8,128)} %get-tuple-element.10.refs_2_, f32[26]{0:T(128)} %bitcast.1), custom_call_target="tpu_custom_call" | custom-call | tf_op jit(solution)/shard_map/hand_out/pallas_call | solution.py:823

commit v4 on v3

--- a/solution.py
+++ b/solution.py
@@ -567,8 +567,6 @@
         total_u[:, p] = total_u[:, p] + step
         grads_1.append(-step)
         values_1.append(mix(backward, -step))
-    sent_h = send_field(4, 1, values_1, inner_h, sides_h, minus_h, plus_h)
-
     grads_2 = [rim_p[:, p + 1, pl.ds(BASE, 8), :] for p in (0, 1)]
     for p in (0, 1):
         total_u[:, p] = total_u[:, p] - grads_2[p]
@@ -617,6 +615,8 @@
     def _():
         along_x[0].start()
 
+    sent_h = send_field(4, 1, values_1, inner_h, sides_h, minus_h, plus_h)
+
     def put_affinity(tile, x, value):
         affinity_out[x, :, 128 * tile : 128 * (tile + 1)] = value.astype(jnp.bfloat16)
 
@@ -624,21 +624,7 @@
     store_a = pltpu.make_async_copy(affinity_out, grad_affinity_hbm, store_sem.at[0])
     store_a.start()
 
-    arrive(sent_h)
     meet(4)
-    gather_field(field_i, inner_h, minus_h, plus_h, 1)
-    sums = message(back_weight_at(0), field_i, (0, 1), 0)
-    for p in (0, 1):
-        current = field_0[1, :, p + 2, pl.ds(BASE, 8), :]
-        total_u[:, p] = total_u[:, p] + softmax_back(current, sums[p])
-
-    def put_unary(tile, x, value):
-        unary_out[x, :, 128 * tile : 128 * (tile + 1)] = value.astype(jnp.bfloat16)
-
-    gather_columns(lambda label, p: total_u[label, p], LABELS // 2, put_unary)
-    store_u = pltpu.make_async_copy(unary_out, grad_unary_hbm, store_sem.at[1])
-    store_u.start()
-
     base = 2 * chips
     along_y = [
         to_peer(gather_b, me_y, base + place, base + place, device)
@@ -658,6 +644,23 @@
         gather_b[me_y] = total
         for copy in along_y:
             copy.start()
+
+    arrive(sent_h)
+    gather_field(field_i, inner_h, minus_h, plus_h, 1)
+    sums = message(back_weight_at(0), field_i, (0, 1), 0)
+    for p in (0, 1):
+        current = field_0[1, :, p + 2, pl.ds(BASE, 8), :]
+        total_u[:, p] = total_u[:, p] + softmax_back(current, sums[p])
+
+    def put_unary(tile, x, value):
+        unary_out[x, :, 128 * tile : 128 * (tile + 1)] = value.astype(jnp.bfloat16)
+
+    gather_columns(lambda label, p: total_u[label, p], LABELS // 2, put_unary)
+    store_u = pltpu.make_async_copy(unary_out, grad_unary_hbm, store_sem.at[1])
+    store_u.start()
+
+    @pl.when(core == 1)
+    def _():
         for copy in along_y:
             copy.wait_recv()
         total = gather_b[0]

time: 47.6 us -> 47.2 us (level)
  no operation moved by 1% of the time
where the time goes in v4:
time: 47.2 us; the launch traced here: 47 us
  Pallas kernels  46.4 us (98%)
  between operations  0.64 us (1%)
    pallas_call x1, Pallas kernels, shards(): pl.pallas_call(functools.partial(kernel, sizes), out_shape=(jax.ShapeDtyp...  44.7 us
    pallas_call x1, Pallas kernels, shards(): pl.pallas_call(hand_out, out_shape=tuple((jax.ShapeDtypeStruct(part.shape...  1.63 us

profile of v4, /device:TPU:1, one launch (start us, length us, event | category | flops | bytes accessed | tf_op | source)
XLA Modules:
  0.0 47.0 jit_solution(1311539187523163962)
XLA Ops:
  0.6 44.7 %mean_field_backward.1 = (bf16[4,8,512]{2,1,0:T(8,128)(2,1)}, bf16[4,8,1664]{2,1,0:T(8,128)(2,1)}, f32[8,8]{1,0:T(8,128)}, f32[1,26]{1,0:T(1,128)}) custom-call(bf16[4,8,512]{2,1,0:T(8,128)(2,1)} %unary_hbm.1, bf16[4,8,1664]{2,1,0:T(8,128)(2,1)} %affinity_hbm.1, bf16[4,8,512]{2,1,0:T(8,128)(2,1)} %cotangent_hbm.1, f32[8,8]{1,0:T(8,128)} %compat_hbm.1, ...), custom_call_target="tpu_custom_call" | custom-call | tf_op jit(solution)/shard_map/mean_field_backward/pallas_call | solution.py:809
  45.4 1.6 %hand_out.1 = (bf16[4,8,512]{2,1,0:T(8,128)(2,1)}, bf16[4,8,1664]{2,1,0:T(8,128)(2,1)}, f32[8,8]{1,0:T(8,128)}, f32[26]{0:T(128)}) custom-call(bf16[4,8,512]{2,1,0:T(8,128)(2,1)} %get-tuple-element.8.refs_0_, bf16[4,8,1664]{2,1,0:T(8,128)(2,1)} %get-tuple-element.9.refs_1_, f32[8,8]{1,0:T(8,128)} %get-tuple-element.10.refs_2_, f32[26]{0:T(128)} %bitcast.1), custom_call_target="tpu_custom_call" | custom-call | tf_op jit(solution)/shard_map/hand_out/pallas_call | solution.py:826

commit v5 on v4

--- a/solution.py
+++ b/solution.py
@@ -206,6 +206,7 @@
         field_h,
         field_i,
         wide_aff,
+        masked_own,
         weight_own,
         weight_rim,
         weight_back,
@@ -327,7 +328,7 @@
         )
 
     def arrive(copies):
-        for copy in copies:
+        for copy in reversed(copies):
             copy.wait_recv()
 
     def narrow(width, reach, inner, sides, box):
@@ -407,6 +408,7 @@
         held[(number, p)] = value
         step_x, step_y, step_z = OFFSETS[number]
         mask = mask_x[p + step_x] * mask_own_y[step_y] * mask_z[step_z]
+        masked_own[number, p] = value * mask
         weight_own[number, p] = value * mask * strength[number]
         if p == 1:
             lay_out(inner_a, sides_a, WIDE, number, held[(number, 0)], value)
@@ -580,13 +582,10 @@
         total = jnp.sum(jnp.sum(total_c[b], axis=1), axis=1, keepdims=True)
         local = jnp.where(lane == 8 * b + sublane, total, local)
     joint_rows = []
-    for number, (step_x, step_y, step_z) in enumerate(OFFSETS):
+    for number in range(NEIGH):
         row = None
         for p in (0, 1):
-            mask = mask_x[p + step_x] * mask_own_y[step_y] * mask_z[step_z]
-            joint = total_r[number, p] * mask
-            total_r[number, p] = joint * strength[number]
-            term = joint * inner_a[inner_rows(0, p, number, WIDE), :]
+            term = total_r[number, p] * masked_own[number, p]
             row = term if row is None else row + term
         joint_rows.append(jnp.sum(row, axis=0, keepdims=True))
     for group in range(4):
@@ -620,7 +619,12 @@
     def put_affinity(tile, x, value):
         affinity_out[x, :, 128 * tile : 128 * (tile + 1)] = value.astype(jnp.bfloat16)
 
-    gather_columns(lambda number, p: total_r[number, p], NEIGH // 2, put_affinity)
+    def own_affinity(number, p):
+        step_x, step_y, step_z = OFFSETS[number]
+        mask = mask_x[p + step_x] * mask_own_y[step_y] * mask_z[step_z]
+        return total_r[number, p] * mask * strength[number]
+
+    gather_columns(own_affinity, NEIGH // 2, put_affinity)
     store_a = pltpu.make_async_copy(affinity_out, grad_affinity_hbm, store_sem.at[0])
     store_a.start()
 
@@ -634,7 +638,7 @@
 
     @pl.when(core == 1)
     def _():
-        for step in range(chips):
+        for step in sorted(range(chips), key=lambda step: ring(step, chips)):
             for sender in (0, 1):
                 if (step, sender) != (0, 1):
                     to_peer(gather_a, me_x, 0, 2 * step + sender, partner).wait_recv()
@@ -659,10 +663,18 @@
     store_u = pltpu.make_async_copy(unary_out, grad_unary_hbm, store_sem.at[1])
     store_u.start()
 
+    for copy in sent_u + sent_a + sent_q + sent_g + sent_h + along_x[1:]:
+        copy.wait_send()
+
+    @pl.when(core == 0)
+    def _():
+        along_x[0].wait_send()
+
     @pl.when(core == 1)
     def _():
         for copy in along_y:
-            copy.wait_recv()
+            copy.wait_send()
+        arrive(along_y)
         total = gather_b[0]
         for place in range(1, size_gy):
             total = total + gather_b[place]
@@ -683,17 +695,9 @@
         table = jnp.where(lane == b, column, table)
     grad_compat[...] = table[:, :LABELS]
 
-    for copy in sent_u + sent_a + sent_q + sent_g + sent_h + along_x[1:]:
-        copy.wait_send()
-
-    @pl.when(core == 0)
-    def _():
-        along_x[0].wait_send()
-
     @pl.when(core == 1)
     def _():
-        for copy in along_y + [to_even]:
-            copy.wait_send()
+        to_even.wait_send()
 
     store_a.wait()
     store_u.wait()
@@ -782,6 +786,7 @@
             field,
             field,
             pltpu.VMEM((NEIGH, 6, TALL, 128), f32),
+            pltpu.VMEM((NEIGH, 2, 8, 128), f32),
             pltpu.VMEM((NEIGH, 2, 8, 128), f32),
             pltpu.VMEM((NEIGH, 4, TALL, 128), f32),
             pltpu.VMEM((NEIGH, 4, TALL, 128), f32),

time: 47.2 us -> 47.1 us (level)
  no operation moved by 1% of the time
where the time goes in v5:
time: 47.1 us; the launch traced here: 46.9 us
  Pallas kernels  46.3 us (98%)
  between operations  0.64 us (1%)
    pallas_call x1, Pallas kernels, shards(): pl.pallas_call(functools.partial(kernel, sizes), out_shape=(jax.ShapeDtyp...  44.6 us
    pallas_call x1, Pallas kernels, shards(): pl.pallas_call(hand_out, out_shape=tuple((jax.ShapeDtypeStruct(part.shape...  1.63 us

profile of v5, /device:TPU:1, one launch (start us, length us, event | category | flops | bytes accessed | tf_op | source)
XLA Modules:
  0.0 46.9 jit_solution(17426295303898457296)
XLA Ops:
  0.6 44.6 %mean_field_backward.1 = (bf16[4,8,512]{2,1,0:T(8,128)(2,1)}, bf16[4,8,1664]{2,1,0:T(8,128)(2,1)}, f32[8,8]{1,0:T(8,128)}, f32[1,26]{1,0:T(1,128)}) custom-call(bf16[4,8,512]{2,1,0:T(8,128)(2,1)} %unary_hbm.1, bf16[4,8,1664]{2,1,0:T(8,128)(2,1)} %affinity_hbm.1, bf16[4,8,512]{2,1,0:T(8,128)(2,1)} %cotangent_hbm.1, f32[8,8]{1,0:T(8,128)} %compat_hbm.1, ...), custom_call_target="tpu_custom_call" | custom-call | tf_op jit(solution)/shard_map/mean_field_backward/pallas_call | solution.py:814
  45.3 1.6 %hand_out.1 = (bf16[4,8,512]{2,1,0:T(8,128)(2,1)}, bf16[4,8,1664]{2,1,0:T(8,128)(2,1)}, f32[8,8]{1,0:T(8,128)}, f32[26]{0:T(128)}) custom-call(bf16[4,8,512]{2,1,0:T(8,128)(2,1)} %get-tuple-element.8.refs_0_, bf16[4,8,1664]{2,1,0:T(8,128)(2,1)} %get-tuple-element.9.refs_1_, f32[8,8]{1,0:T(8,128)} %get-tuple-element.10.refs_2_, f32[26]{0:T(128)} %bitcast.1), custom_call_target="tpu_custom_call" | custom-call | tf_op jit(solution)/shard_map/hand_out/pallas_call | solution.py:831

commit v6 on v5

--- a/solution.py
+++ b/solution.py
@@ -244,9 +244,6 @@
         pltpu.make_async_copy(strength_hbm, strength, load_sem.at[3]),
         pltpu.make_async_copy(compat_hbm, compat, load_sem.at[4]),
     ]
-    for load in loads:
-        load.start()
-
     neighbours = [
         (around(me_x, step_x, size_gx), around(me_y, step_y, size_gy))
         for step_x, step_y in DIRECTIONS
@@ -273,6 +270,8 @@
             pl.semaphore_signal(barrier, inc=1, device_id=device, device_id_type=MESH)
 
     greet(neighbours)
+    for load in loads:
+        load.start()
 
     rounds = [doubling(size_gx), doubling(size_gy)]
 
@@ -420,12 +419,11 @@
     narrow(LABELS, 1, inner_u, sides_u, box_u)
     narrow(WIDE, 2, inner_a, sides_a, box_a)
     pl.semaphore_wait(barrier, len(neighbours))
-    meet(0)
     sent_u = start_narrow(0, 1, box_u)
     sent_a = start_narrow(1, 2, box_a)
+    meet(0)
 
     arrive_narrow(sent_u, LABELS, 1, inner_u, minus_u, plus_u, box_u)
-    meet(1)
     for label in range(LABELS):
         for y in (-1, 1):
             found = assemble(inner_u, minus_u, plus_u, LABELS, label, y, 1)
@@ -462,6 +460,7 @@
         message_1[:, p] = sums[p]
         values.append(normalise(own_logits(p) - mix(forward, sums[p])))
     sent_q = send_field(2, 2, values, inner_q, sides_q, minus_q, plus_q)
+    meet(1)
 
     loads[2].wait()
 
@@ -500,7 +499,6 @@
     rim_weights(weight_rim, rim_value)
 
     arrive(sent_q)
-    meet(2)
     gather_field(field_1, inner_q, minus_q, plus_q, 2)
     for y in (-1, 1):
 
@@ -525,6 +523,7 @@
     lay_field(values, inner_g, sides_g)
     narrow(LABELS, 2, inner_g, sides_g, box_g)
     sent_g = start_narrow(3, 2, box_g)
+    meet(2)
 
     def add_compat(grads, messages, begin):
         for b in range(LABELS):

time: 47.1 us -> 47 us (level)
  no operation moved by 1% of the time
where the time goes in v6:
time: 47 us; the launch traced here: 46.9 us
  Pallas kernels  46.2 us (98%)
  between operations  0.64 us (1%)
    pallas_call x1, Pallas kernels, shards(): pl.pallas_call(functools.partial(kernel, sizes), out_shape=(jax.ShapeDtyp...  44.6 us
    pallas_call x1, Pallas kernels, shards(): pl.pallas_call(hand_out, out_shape=tuple((jax.ShapeDtypeStruct(part.shape...  1.63 us

profile of v6, /device:TPU:1, one launch (start us, length us, event | category | flops | bytes accessed | tf_op | source)
XLA Modules:
  0.0 46.9 jit_solution(11238869264884976074)
XLA Ops:
  0.6 44.6 %mean_field_backward.1 = (bf16[4,8,512]{2,1,0:T(8,128)(2,1)}, bf16[4,8,1664]{2,1,0:T(8,128)(2,1)}, f32[8,8]{1,0:T(8,128)}, f32[1,26]{1,0:T(1,128)}) custom-call(bf16[4,8,512]{2,1,0:T(8,128)(2,1)} %unary_hbm.1, bf16[4,8,1664]{2,1,0:T(8,128)(2,1)} %affinity_hbm.1, bf16[4,8,512]{2,1,0:T(8,128)(2,1)} %cotangent_hbm.1, f32[8,8]{1,0:T(8,128)} %compat_hbm.1, ...), custom_call_target="tpu_custom_call" | custom-call | tf_op jit(solution)/shard_map/mean_field_backward/pallas_call | solution.py:813
  45.2 1.6 %hand_out.1 = (bf16[4,8,512]{2,1,0:T(8,128)(2,1)}, bf16[4,8,1664]{2,1,0:T(8,128)(2,1)}, f32[8,8]{1,0:T(8,128)}, f32[26]{0:T(128)}) custom-call(bf16[4,8,512]{2,1,0:T(8,128)(2,1)} %get-tuple-element.8.refs_0_, bf16[4,8,1664]{2,1,0:T(8,128)(2,1)} %get-tuple-element.9.refs_1_, f32[8,8]{1,0:T(8,128)} %get-tuple-element.10.refs_2_, f32[26]{0:T(128)} %bitcast.1), custom_call_target="tpu_custom_call" | custom-call | tf_op jit(solution)/shard_map/hand_out/pallas_call | solution.py:830
